TPU v7x, 32 devices: a whole 2x2x4 slice. The times are simulated.
32 devices in a mesh: groups: 2 (over x), rows: 16 (over z, y, core).
Axes of the slice: x: 2, y: 2, z: 4, core: 2. Of those that a mesh axis runs over, the one named last changes fastest.
Arguments:
- features: bfloat16 [128, 4, 3072], P(('groups', 'rows')), parts along dimension 0, may hold values from -6 to 6
- cotangent: bfloat16 [128, 4, 3072], P(('groups', 'rows')), parts along dimension 0, may hold values from -6 to 6
- depth_kernel: float32 [7, 7, 3072], replicated, may hold values from -0.875 to 0.875
- depth_bias: float32 [3072], replicated, may hold values from -3 to 3
- norm_gain: float32 [3072], replicated, may hold values from 0.1 to 1.9
- norm_shift: float32 [3072], replicated, may hold values from -3 to 3
- up_weight: bfloat16 [3072, 12288], P(None, 'rows'), may hold values from -0.109375 to 0.109375
- up_bias: float32 [12288], P('rows'), may hold values from -3 to 3
- down_weight: bfloat16 [12288, 3072], P('rows'), may hold values from -0.109375 to 0.109375
- layer_scale: float32 [3072], replicated, may hold values from 0.3 to 3
Outputs:
- input_grad: bfloat16 [128, 4, 3072], P(('groups', 'rows')), parts along dimension 0
- up_grad: float32 [6144, 12288], P('groups', 'rows'), parts along dimension 0
- up_bias_grad: float32 [24576], P(('groups', 'rows')), parts along dimension 0
- down_grad: float32 [24576, 3072], P(('groups', 'rows')), parts along dimension 0
- kernel_grad: float32 [14, 7, 3072], P('groups'), parts along dimension 0
- depth_bias_grad: float32 [6144], P('groups'), parts along dimension 0
- gain_grad: float32 [6144], P('groups'), parts along dimension 0
- shift_grad: float32 [6144], P('groups'), parts along dimension 0
There are 2 independent parts, one for each index of `groups`. A program takes and returns all parts, laid end to end along the dimension named above; an argument that names none is the same for every part. Nothing has to cross between parts.
All inputs are finite; a program needn't handle non-finite values.
Results may differ from a plain program's by a relative error of at most 0.0075.
Values may be sent and summed in bfloat16 or wider, within the bound.
No kernel may reach another device: no remote copies, remote signals or barrier semaphores. Data moves between devices by JAX's collectives and lax.ppermute only.
A program may use at most 128 MiB of HBM per device.

v0:
```python
import jax
import jax.numpy as jnp
from jax import lax
from jax.sharding import PartitionSpec as P

IMG_ROWS = 32


def extended(cells, sides, width):
    for axis, dim in sides:
        count = lax.axis_size(axis)
        head = lax.slice_in_dim(cells, 0, width, axis=dim)
        tail = lax.slice_in_dim(cells, cells.shape[dim] - width, cells.shape[dim], axis=dim)
        cells = jnp.concatenate(
            [
                lax.ppermute(tail, axis, [(i, (i + 1) % count) for i in range(count)]),
                cells,
                lax.ppermute(head, axis, [((i + 1) % count, i) for i in range(count)]),
            ],
            axis=dim,
        )
    return cells


def gelu_value(pre_act):
    return 0.5 * pre_act * (1.0 + jax.scipy.special.erf(pre_act * 0.7071067811865476))


def gelu_slope(pre_act):
    cdf_part = 0.5 * (1.0 + jax.scipy.special.erf(pre_act * 0.7071067811865476))
    return cdf_part + pre_act * jnp.exp(-0.5 * pre_act * pre_act) * 0.3989422804014327


def contract(left, right, left_dim, right_dim):
    return lax.dot_general(
        left, right, (((left_dim,), (right_dim,)), ((), ())), preferred_element_type=jnp.float32
    )


def depthwise(padded, kernel, offset_term, row_count, col_count):
    summed = jnp.zeros(padded[..., 3 : 3 + row_count, 3 : 3 + col_count, :].shape, padded.dtype)
    for tap_row in range(7):
        for tap_col in range(7):
            summed = (
                summed
                + kernel[tap_row, tap_col]
                * padded[..., tap_row : tap_row + row_count, tap_col : tap_col + col_count, :]
            )
    return summed + offset_term


def depthwise_back(padded_grad, kernel, row_count, col_count):
    summed = jnp.zeros(
        padded_grad[..., 3 : 3 + row_count, 3 : 3 + col_count, :].shape, padded_grad.dtype
    )
    for tap_row in range(7):
        for tap_col in range(7):
            summed = (
                summed
                + kernel[tap_row, tap_col]
                * padded_grad[
                    ...,
                    6 - tap_row : 6 - tap_row + row_count,
                    6 - tap_col : 6 - tap_col + col_count,
                    :,
                ]
            )
    return summed


def normalize(conv_out):
    row_mean = jnp.mean(conv_out, axis=-1, keepdims=True)
    centred = conv_out - row_mean
    inv_std = lax.rsqrt(jnp.mean(centred * centred, axis=-1, keepdims=True) + 1e-06)
    return (centred * inv_std, inv_std)


def norm_back(norm_grad, unit_norm, inv_std, norm_gain):
    scaled = norm_grad * norm_gain
    return inv_std * (
        scaled
        - jnp.mean(scaled, axis=-1, keepdims=True)
        - unit_norm * jnp.mean(scaled * unit_norm, axis=-1, keepdims=True)
    )


def pad_columns(block):
    return jnp.pad(block, ((0, 0), (3, 3), (0, 0)))


def on_device(
    features,
    cotangent,
    depth_kernel,
    depth_bias,
    norm_gain,
    norm_shift,
    up_weight,
    up_bias,
    down_weight,
    layer_scale,
):
    rows_dev, col_count, channels = features.shape
    total_rows = rows_dev * lax.axis_size("rows")
    half_image = IMG_ROWS // 2
    my_index = lax.axis_index("rows")
    first_row = my_index * rows_dev
    row_offsets = first_row - 3 + jnp.arange(rows_dev + 6, dtype=jnp.int32)
    row_image = jnp.mod(row_offsets - half_image, total_rows) // IMG_ROWS
    own_image = jnp.mod(first_row - half_image, total_rows) // IMG_ROWS
    row_mask = (row_image == own_image).astype(jnp.float32)[:, None, None]
    cot_scaled = (
        (cotangent.astype(jnp.float32) * layer_scale)
        .astype(jnp.bfloat16)
        .reshape(rows_dev * col_count, channels)
    )
    cot_all = lax.all_gather(cot_scaled, "rows", axis=0, tiled=True)
    near_rows = extended(features, (("rows", 0),), 3)
    padded = pad_columns(near_rows.astype(jnp.float32) * row_mask)
    conv_out = depthwise(padded, depth_kernel, depth_bias, rows_dev, col_count)
    unit_norm, inv_std = normalize(conv_out)
    normed = (
        (unit_norm * norm_gain + norm_shift)
        .astype(jnp.bfloat16)
        .reshape(rows_dev * col_count, channels)
    )
    normed_all = lax.all_gather(normed, "rows", axis=0, tiled=True)
    pre_act = jnp.dot(normed_all, up_weight, preferred_element_type=jnp.float32) + up_bias
    hidden = gelu_value(pre_act).astype(jnp.bfloat16)
    down_grad = contract(hidden, cot_all, 0, 0)
    hid_grad = contract(cot_all, down_weight, 1, 1)
    act_grad = (hid_grad * gelu_slope(pre_act)).astype(jnp.bfloat16)
    up_bias_grad = jnp.sum(act_grad.astype(jnp.float32), axis=0)
    up_grad = contract(normed_all, act_grad, 0, 0)
    norm_grad = lax.psum_scatter(
        contract(act_grad, up_weight, 1, 1), "rows", scatter_dimension=0, tiled=True
    ).reshape(rows_dev, col_count, channels)
    gain_part = jnp.sum(norm_grad * unit_norm, axis=(0, 1))
    shift_part = jnp.sum(norm_grad, axis=(0, 1))
    conv_grad = norm_back(norm_grad, unit_norm, inv_std, norm_gain)
    bias_part = jnp.sum(conv_grad, axis=(0, 1))
    kernel_rows = []
    for tap_row in range(7):
        kernel_cols = []
        for tap_col in range(7):
            kernel_cols.append(
                jnp.sum(
                    conv_grad
                    * padded[tap_row : tap_row + rows_dev, tap_col : tap_col + col_count, :],
                    axis=(0, 1),
                )
            )
        kernel_rows.append(jnp.stack(kernel_cols))
    kernel_part = jnp.stack(kernel_rows)
    near_grad = extended(conv_grad.astype(jnp.bfloat16), (("rows", 0),), 3).astype(conv_grad.dtype)
    grad_padded = pad_columns(near_grad * row_mask)
    back_term = depthwise_back(grad_padded, depth_kernel, rows_dev, col_count)
    input_grad = (cotangent.astype(jnp.float32) + back_term).astype(jnp.bfloat16)
    gain_grad, shift_grad, kernel_grad, depth_bias_grad = lax.psum(
        (gain_part, shift_part, kernel_part, bias_part), "rows"
    )
    return (
        input_grad,
        up_grad,
        up_bias_grad,
        down_grad,
        kernel_grad,
        depth_bias_grad,
        gain_grad,
        shift_grad,
    )


def solution(mesh):
    in_specs = (
        P(("groups", "rows"), None, None),
        P(("groups", "rows"), None, None),
        P(),
        P(),
        P(),
        P(),
        P(None, "rows"),
        P("rows"),
        P("rows", None),
        P(),
    )
    out_specs = (
        P(("groups", "rows"), None, None),
        P("groups", "rows"),
        P(("groups", "rows")),
        P(("groups", "rows"), None),
        P("groups", None, None),
        P("groups"),
        P("groups"),
        P("groups"),
    )
    return jax.shard_map(
        on_device, mesh=mesh, in_specs=in_specs, out_specs=out_specs, check_vma=False
    )
```

profile of v0, /device:TPU:0, one launch (start us, length us, event | category | flops | bytes accessed | tf_op | source)
XLA Modules:
  0.0 296.4 jit_solution(8445374431140622717)
XLA Ops:
  7.2 0.0 all-gather.5.cloned.1.call-start
  7.2 1.0 fusion.107
  8.2 0.5 collective-permute-start
  8.7 5.1 %collective-permute-start.1 = (bf16[3,4,3072]{2,1,0:T(4,128)(2,1)S(1)}, bf16[3,4,3072]{2,1,0:T(4,128)(2,1)S(1)}, u32[]{:S(2)}, u32[]{:S(2)}) collective-permute-start(bf16[3,4,3072]{2,1,0:T(4,128)(2,1)S(1)} %get-tuple-element.121), channel_id=1, source_target_pairs={{1,0},{2,1},{3,2},{4,3},{5,4},{6,5},{7,6},{8,7},{9,8},{10,9},{11,1... | collective-permute-start | bytes 221192 | tf_op jit(solution)/shard_map/ppermute | solution.py:18
  13.8 1.7 fusion.105
  15.6 2.3 fusion.103
  17.9 0.0 copy-start.27
  18.1 2.8 fusion.104
  20.9 0.0 copy-start.4
  21.0 0.0 copy-start.86
  21.0 0.6 compare_convert_fusion
  21.6 0.0 collective-permute-done
  21.6 0.0 collective-permute-done.1
  21.6 1.1 convert_multiply_fusion.1
  22.7 0.0 copy-start.3
  22.7 0.0 copy-start.87
  22.7 0.0 copy-start.88
  22.7 5.2 %fusion.102 = (f32[4,4]{1,0:T(4,128)S(1)}, f32[4,4,3072]{2,1,0:T(4,128)S(1)}) fusion(f32[3072]{0:T(1024)S(1)} %copy-done.85, f32[3072]{0:T(1024)S(1)} %bitcast.139, f32[3072]{0:T(1024)S(1)} %bitcast.141, f32[3072]{0:T(1024)S(1)} %bitcast.145, f32[10,4,3072]{2,1,0:T(4,128)S(1)} %convert_multiply_fusion.1, f32[3072]{0:T(1024)S(1)} %bitcast.147, ...), kind=kLoop, calls=%fused_computation.279 | loop fusion | flops 4866032 | bytes 2678848 | tf_op jit(solution)/shard_map/reduce_sum | solution.py:72
  28.3 0.2 multiply_reduce_fusion.52
  28.5 0.0 copy-start.83
  28.5 0.1 add_convert_fusion
  28.8 0.7 reshape.90
  29.4 0.0 all-gather.5.cloned.1.call-update
  29.5 0.0 all-gather.3.cloned.1.call-start
  29.6 0.7 reshape.89
  30.2 0.0 all-gather.3.cloned.1.call-update
  30.3 0.0 reduce-scatter.2.cloned.1.call-start
  30.3 37.9 %all-gather.5.cloned.1.call-done = bf16[256,3072]{1,0:T(8,128)(2,1)} async-done(((bf16[16,3072]{1,0:T(8,128)(2,1)}), bf16[256,3072]{1,0:T(8,128)(2,1)}) %all-gather.5.cloned.1.call-update) | async-done | bytes 1572880 | tf_op jit(solution)/shard_map/all_gather | solution.py:127
  68.2 4.2 %convolution_add_fusion = f32[256,768]{1,0:T(8,128)S(1)} fusion(bf16[256,3072]{1,0:T(8,128)(2,1)} %all-gather.5.cloned.1.call-done, bf16[3072,768]{1,0:T(8,128)(2,1)} %param.16, f32[768]{0:T(1024)S(1)} %copy-done.88), kind=kOutput, calls=%fused_computation.85 | convolution fusion | flops 1208156160 | bytes 7080960 | tf_op jit(solution)/shard_map/dot_general | solution.py:128
  72.4 37.2 %all-gather.3.cloned.1.call-done = bf16[256,3072]{1,0:T(8,128)(2,1)} async-done(((bf16[16,3072]{1,0:T(8,128)(2,1)}), bf16[256,3072]{1,0:T(8,128)(2,1)}) %all-gather.3.cloned.1.call-update) | async-done | bytes 1572880 | tf_op jit(solution)/shard_map/all_gather | solution.py:117
  109.7 5.0 %convert_reduce_fusion = (f32[768]{0:T(1024)}, bf16[256,768]{1,0:T(8,128)(2,1)S(1)}) fusion(f32[256,768]{1,0:T(8,128)S(1)} %convolution_add_fusion, bf16[256,3072]{1,0:T(8,128)(2,1)} %all-gather.3.cloned.1.call-done, bf16[768,3072]{1,0:T(8,128)(2,1)} %param.18), kind=kOutput, calls=%fused_computation.93 | convolution fusion | flops 1210318080 | bytes 7474176 | tf_op jit(solution)/shard_map/dot_general | solution.py:35
  114.6 5.4 %fusion.108 = f32[256,3072]{1,0:T(8,128)} fusion(bf16[256,768]{1,0:T(8,128)(2,1)S(1)} %get-tuple-element.123, bf16[3072,768]{1,0:T(8,128)(2,1)} %param.16), kind=kOutput, calls=%fused_computation.285 | convolution fusion | flops 1207959552 | bytes 8257536 | tf_op jit(solution)/shard_map/dot_general | solution.py:35
  120.1 0.0 reduce-scatter.2.cloned.1.call-update
  120.1 0.2 all-reduce.5.cloned.1.call-start
  120.3 1.2 copy-done
  121.5 5.2 %fusion.109 = f32[3072,768]{1,0:T(8,128)} fusion(bf16[256,3072]{1,0:T(8,128)(2,1)S(1)} %copy-done, bf16[256,768]{1,0:T(8,128)(2,1)S(1)} %get-tuple-element.123), kind=kOutput, calls=%fused_computation.286 | convolution fusion | flops 1207959552 | bytes 11403264 | tf_op jit(solution)/shard_map/dot_general | solution.py:35
  126.7 5.2 %fusion.5 = f32[768,3072]{1,0:T(8,128)} fusion(bf16[256,3072]{1,0:T(8,128)(2,1)S(1)} %copy-done.1, f32[256,768]{1,0:T(8,128)S(1)} %convolution_add_fusion), kind=kOutput, calls=%fused_computation.97 | convolution fusion | flops 1208942592 | bytes 11796480 | tf_op jit(solution)/shard_map/dot_general | solution.py:35
  131.9 53.5 %reduce-scatter.2.cloned.1.call-done = f32[16,3072]{1,0:T(8,128)} async-done(((f32[256,3072]{1,0:T(8,128)}), f32[16,3072]{1,0:T(8,128)}) %reduce-scatter.2.cloned.1.call-update) | async-done | bytes 196624 | tf_op jit(solution)/shard_map/reduce_scatter | solution.py:135
  185.4 1.1 fusion.101
  186.4 0.1 div.44
  186.5 1.0 reshape.91
  187.5 0.3 multiply_reduce_fusion
  187.8 1.5 multiply_reduce_fusion.1
  189.3 1.0 multiply_reduce_fusion.37
  190.3 1.3 multiply_reduce_fusion.19
  191.7 0.1 collective-permute-start.2
  191.8 4.4 %collective-permute-start.3 = (bf16[3,4,3072]{2,1,0:T(4,128)(2,1)S(1)}, bf16[3,4,3072]{2,1,0:T(4,128)(2,1)S(1)}, u32[]{:S(2)}, u32[]{:S(2)}) collective-permute-start(bf16[3,4,3072]{2,1,0:T(4,128)(2,1)S(1)} %get-tuple-element.119), channel_id=1, source_target_pairs={{1,0},{2,1},{3,2},{4,3},{5,4},{6,5},{7,6},{8,7},{9,8},{10,9},{11,1... | collective-permute-start | bytes 221192 | tf_op jit(solution)/shard_map/ppermute | solution.py:18
  196.2 0.1 stack.199
  196.7 0.1 stack.208
  196.9 0.1 stack.217
  197.1 0.1 stack.226
  197.2 0.1 stack.235
  197.4 0.1 stack.244
  197.5 0.1 stack.253
  197.7 0.0 copy-start.2
  197.7 0.8 copy-done.2
  198.5 0.0 all-reduce.5.cloned.1.call-update
  198.6 58.5 %all-reduce.2 = (f32[3072]{0:T(1024)}, f32[3072]{0:T(1024)}, f32[3072]{0:T(1024)}) all-reduce(f32[3072]{0:T(1024)S(1)} %get-tuple-element.61, f32[3072]{0:T(1024)S(1)} %get-tuple-element.57, f32[3072]{0:T(1024)S(1)} %get-tuple-element.59), channel_id=1, replica_groups=mesh['groups'=2,'rows'=16] {'rows'}, use_global_device_ids=true, to_apply=%region_57.58 | all-reduce | flops 9216 | bytes 73728 | tf_op jit(solution)/shard_map/psum | solution.py:159
  257.1 0.0 collective-permute-done.2
  257.1 0.0 collective-permute-done.3
  257.1 0.9 convert_multiply_fusion
  258.3 4.2 %fusion.8 = bf16[4,4,3072]{2,1,0:T(4,128)(2,1)} fusion(bf16[4,4,3072]{2,1,0:T(4,128)(2,1)S(1)} %copy-done.3, f32[10,4,3072]{2,1,0:T(4,128)S(1)} %convert_multiply_fusion, f32[3072]{0:T(1024)S(1)} %bitcast.140, f32[3072]{0:T(1024)S(1)} %bitcast.142, f32[3072]{0:T(1024)S(1)} %bitcast.146, f32[3072]{0:T(1024)S(1)} %bitcast.148, f32[3072]{0:T(1024)S(1)} %bitcast.150, ...), kind=kLoop, calls=%fused_computation.102 | loop fusion | flops 4915200 | bytes 2666496 | tf_op jit(solution)/shard_map/convert_element_type | solution.py:158
  262.6 25.3 %all-reduce.5.cloned.1.call-done = f32[7,7,3072]{2,1,0:T(8,128)} async-done(((f32[7,7,3072]{2,1,0:T(8,128)}), f32[7,7,3072]{2,1,0:T(8,128)}) %all-reduce.5.cloned.1.call-update) | async-done | bytes 602128 | tf_op jit(solution)/shard_map/psum | solution.py:159
  287.9 2.0 copy.25
  (181 shorter events, 0.5 us)
Async XLA Ops:
  7.2 15.5 %copy-start.85 = (f32[3072]{0:T(1024)S(1)}, f32[3072]{0:T(1024)}, u32[]{:S(2)}) copy-start(f32[3072]{0:T(1024)} %param.13) | copy-start | bytes 36868
  7.2 61.0 %all-gather.5.cloned.1.call-start = ((), (), s32[]{:S(2)}) async-start(), calls=%async_computation.2 | async-start | bytes 1671168 | tf_op jit(solution)/shard_map/all_gather | solution.py:127
  8.2 13.4 %collective-permute-start = (bf16[3,4,3072]{2,1,0:T(4,128)(2,1)S(1)}, bf16[3,4,3072]{2,1,0:T(4,128)(2,1)S(1)}, u32[]{:S(2)}, u32[]{:S(2)}) collective-permute-start(bf16[3,4,3072]{2,1,0:T(4,128)(2,1)S(1)} %get-tuple-element.120), channel_id=1, source_target_pairs={{0,1},{1,2},{2,3},{3,4},{4,5},{5,6},{6,7},{7,8},{8,9},{9,10},{10,1... | collective-permute-start | bytes 221192 | tf_op jit(solution)/shard_map/ppermute | solution.py:16
  8.7 12.9 %collective-permute-start.1 = (bf16[3,4,3072]{2,1,0:T(4,128)(2,1)S(1)}, bf16[3,4,3072]{2,1,0:T(4,128)(2,1)S(1)}, u32[]{:S(2)}, u32[]{:S(2)}) collective-permute-start(bf16[3,4,3072]{2,1,0:T(4,128)(2,1)S(1)} %get-tuple-element.121), channel_id=1, source_target_pairs={{1,0},{2,1},{3,2},{4,3},{5,4},{6,5},{7,6},{8,7},{9,8},{10,9},{11,1... | collective-permute-start | bytes 221192 | tf_op jit(solution)/shard_map/ppermute | solution.py:18
  15.5 12.5 %copy-start.5 = (f32[1,1,3072]{2,1,0:T(1,128)}, f32[1,1,3072]{2,1,0:T(1,128)S(1)}, u32[]{:S(2)}) copy-start(f32[1,1,3072]{2,1,0:T(1,128)S(1)} %get-tuple-element.106) | copy-start | bytes 36868
  15.5 12.5 %copy-start.7 = (f32[1,1,3072]{2,1,0:T(1,128)}, f32[1,1,3072]{2,1,0:T(1,128)S(1)}, u32[]{:S(2)}) copy-start(f32[1,1,3072]{2,1,0:T(1,128)S(1)} %get-tuple-element.107) | copy-start | bytes 36868
  15.5 12.5 %copy-start.9 = (f32[1,1,3072]{2,1,0:T(1,128)}, f32[1,1,3072]{2,1,0:T(1,128)S(1)}, u32[]{:S(2)}) copy-start(f32[1,1,3072]{2,1,0:T(1,128)S(1)} %get-tuple-element.108) | copy-start | bytes 36868
  15.5 12.5 %copy-start.11 = (f32[1,1,3072]{2,1,0:T(1,128)}, f32[1,1,3072]{2,1,0:T(1,128)S(1)}, u32[]{:S(2)}) copy-start(f32[1,1,3072]{2,1,0:T(1,128)S(1)} %get-tuple-element.109) | copy-start | bytes 36868
  15.5 12.5 %copy-start.13 = (f32[1,1,3072]{2,1,0:T(1,128)}, f32[1,1,3072]{2,1,0:T(1,128)S(1)}, u32[]{:S(2)}) copy-start(f32[1,1,3072]{2,1,0:T(1,128)S(1)} %get-tuple-element.110) | copy-start | bytes 36868
  15.5 12.5 %copy-start.15 = (f32[1,1,3072]{2,1,0:T(1,128)}, f32[1,1,3072]{2,1,0:T(1,128)S(1)}, u32[]{:S(2)}) copy-start(f32[1,1,3072]{2,1,0:T(1,128)S(1)} %get-tuple-element.111) | copy-start | bytes 36868
  15.5 12.5 %copy-start.17 = (f32[1,1,3072]{2,1,0:T(1,128)}, f32[1,1,3072]{2,1,0:T(1,128)S(1)}, u32[]{:S(2)}) copy-start(f32[1,1,3072]{2,1,0:T(1,128)S(1)} %get-tuple-element.112) | copy-start | bytes 36868
  15.5 12.5 %copy-start.19 = (f32[1,1,3072]{2,1,0:T(1,128)}, f32[1,1,3072]{2,1,0:T(1,128)S(1)}, u32[]{:S(2)}) copy-start(f32[1,1,3072]{2,1,0:T(1,128)S(1)} %get-tuple-element.113) | copy-start | bytes 36868
  15.6 12.5 %copy-start.21 = (f32[1,1,3072]{2,1,0:T(1,128)}, f32[1,1,3072]{2,1,0:T(1,128)S(1)}, u32[]{:S(2)}) copy-start(f32[1,1,3072]{2,1,0:T(1,128)S(1)} %get-tuple-element.114) | copy-start | bytes 36868
  15.6 12.5 %copy-start.23 = (f32[1,1,3072]{2,1,0:T(1,128)}, f32[1,1,3072]{2,1,0:T(1,128)S(1)}, u32[]{:S(2)}) copy-start(f32[1,1,3072]{2,1,0:T(1,128)S(1)} %get-tuple-element.115) | copy-start | bytes 36868
  15.6 12.5 %copy-start.25 = (f32[1,1,3072]{2,1,0:T(1,128)}, f32[1,1,3072]{2,1,0:T(1,128)S(1)}, u32[]{:S(2)}) copy-start(f32[1,1,3072]{2,1,0:T(1,128)S(1)} %get-tuple-element.116) | copy-start | bytes 36868
  17.9 10.2 %copy-start.27 = (f32[1,1,3072]{2,1,0:T(1,128)}, f32[1,1,3072]{2,1,0:T(1,128)S(1)}, u32[]{:S(2)}) copy-start(f32[1,1,3072]{2,1,0:T(1,128)S(1)} %get-tuple-element.68) | copy-start | bytes 36868
  17.9 10.2 %copy-start.29 = (f32[1,1,3072]{2,1,0:T(1,128)}, f32[1,1,3072]{2,1,0:T(1,128)S(1)}, u32[]{:S(2)}) copy-start(f32[1,1,3072]{2,1,0:T(1,128)S(1)} %get-tuple-element.69) | copy-start | bytes 36868
  17.9 10.2 %copy-start.31 = (f32[1,1,3072]{2,1,0:T(1,128)}, f32[1,1,3072]{2,1,0:T(1,128)S(1)}, u32[]{:S(2)}) copy-start(f32[1,1,3072]{2,1,0:T(1,128)S(1)} %get-tuple-element.70) | copy-start | bytes 36868
  22.7 45.5 %copy-start.88 = (f32[768]{0:T(1024)S(1)}, f32[768]{0:T(1024)}, u32[]{:S(2)}) copy-start(f32[768]{0:T(1024)} %param.17) | copy-start | bytes 9220
  29.5 80.2 %all-gather.3.cloned.1.call-start = ((), (), s32[]{:S(2)}) async-start(), calls=%async_computation.1 | async-start | bytes 1671168 | tf_op jit(solution)/shard_map/all_gather | solution.py:117
  30.3 155.1 %reduce-scatter.2.cloned.1.call-start = ((), (), s32[]{:S(2)}) async-start(), calls=%async_computation.3 | async-start | bytes 3342336 | tf_op jit(solution)/shard_map/reduce_scatter | solution.py:135
  120.1 167.8 %all-reduce.5.cloned.1.call-start = ((), (), s32[]{:S(2)}) async-start(), calls=%async_computation.4 | async-start | bytes 1376256 | tf_op jit(solution)/shard_map/psum | solution.py:159
  126.7 60.8 %copy-start.84 = (f32[4,4]{1,0:T(4,128)S(1)}, f32[4,4]{1,0:T(4,128)}, u32[]{:S(2)}) copy-start(f32[4,4]{1,0:T(4,128)} %copy-done.83) | copy-start | bytes 196
  191.7 65.4 %collective-permute-start.2 = (bf16[3,4,3072]{2,1,0:T(4,128)(2,1)S(1)}, bf16[3,4,3072]{2,1,0:T(4,128)(2,1)S(1)}, u32[]{:S(2)}, u32[]{:S(2)}) collective-permute-start(bf16[3,4,3072]{2,1,0:T(4,128)(2,1)S(1)} %get-tuple-element.118), channel_id=1, source_target_pairs={{0,1},{1,2},{2,3},{3,4},{4,5},{5,6},{6,7},{7,8},{8,9},{9,10},{10,1... | collective-permute-start | bytes 221192 | tf_op jit(solution)/shard_map/ppermute | solution.py:16
  191.8 65.3 %collective-permute-start.3 = (bf16[3,4,3072]{2,1,0:T(4,128)(2,1)S(1)}, bf16[3,4,3072]{2,1,0:T(4,128)(2,1)S(1)}, u32[]{:S(2)}, u32[]{:S(2)}) collective-permute-start(bf16[3,4,3072]{2,1,0:T(4,128)(2,1)S(1)} %get-tuple-element.119), channel_id=1, source_target_pairs={{1,0},{2,1},{3,2},{4,3},{5,4},{6,5},{7,6},{8,7},{9,8},{10,9},{11,1... | collective-permute-start | bytes 221192 | tf_op jit(solution)/shard_map/ppermute | solution.py:18
  196.4 61.6 %copy-start.6 = (f32[1,1,3072]{2,1,0:T(1,128)S(1)}, f32[1,1,3072]{2,1,0:T(1,128)}, u32[]{:S(2)}) copy-start(f32[1,1,3072]{2,1,0:T(1,128)} %copy-done.5) | copy-start | bytes 36868
  196.4 61.6 %copy-start.8 = (f32[1,1,3072]{2,1,0:T(1,128)S(1)}, f32[1,1,3072]{2,1,0:T(1,128)}, u32[]{:S(2)}) copy-start(f32[1,1,3072]{2,1,0:T(1,128)} %copy-done.7) | copy-start | bytes 36868
  196.4 61.6 %copy-start.10 = (f32[1,1,3072]{2,1,0:T(1,128)S(1)}, f32[1,1,3072]{2,1,0:T(1,128)}, u32[]{:S(2)}) copy-start(f32[1,1,3072]{2,1,0:T(1,128)} %copy-done.9) | copy-start | bytes 36868
  196.4 61.6 %copy-start.12 = (f32[1,1,3072]{2,1,0:T(1,128)S(1)}, f32[1,1,3072]{2,1,0:T(1,128)}, u32[]{:S(2)}) copy-start(f32[1,1,3072]{2,1,0:T(1,128)} %copy-done.11) | copy-start | bytes 36868
  196.4 61.6 %copy-start.14 = (f32[1,1,3072]{2,1,0:T(1,128)S(1)}, f32[1,1,3072]{2,1,0:T(1,128)}, u32[]{:S(2)}) copy-start(f32[1,1,3072]{2,1,0:T(1,128)} %copy-done.13) | copy-start | bytes 36868
  196.4 61.6 %copy-start.16 = (f32[1,1,3072]{2,1,0:T(1,128)S(1)}, f32[1,1,3072]{2,1,0:T(1,128)}, u32[]{:S(2)}) copy-start(f32[1,1,3072]{2,1,0:T(1,128)} %copy-done.15) | copy-start | bytes 36868
  196.4 61.6 %copy-start.18 = (f32[1,1,3072]{2,1,0:T(1,128)S(1)}, f32[1,1,3072]{2,1,0:T(1,128)}, u32[]{:S(2)}) copy-start(f32[1,1,3072]{2,1,0:T(1,128)} %copy-done.17) | copy-start | bytes 36868
  196.4 61.6 %copy-start.20 = (f32[1,1,3072]{2,1,0:T(1,128)S(1)}, f32[1,1,3072]{2,1,0:T(1,128)}, u32[]{:S(2)}) copy-start(f32[1,1,3072]{2,1,0:T(1,128)} %copy-done.19) | copy-start | bytes 36868
  196.4 61.6 %copy-start.22 = (f32[1,1,3072]{2,1,0:T(1,128)S(1)}, f32[1,1,3072]{2,1,0:T(1,128)}, u32[]{:S(2)}) copy-start(f32[1,1,3072]{2,1,0:T(1,128)} %copy-done.21) | copy-start | bytes 36868
  196.4 61.6 %copy-start.24 = (f32[1,1,3072]{2,1,0:T(1,128)S(1)}, f32[1,1,3072]{2,1,0:T(1,128)}, u32[]{:S(2)}) copy-start(f32[1,1,3072]{2,1,0:T(1,128)} %copy-done.23) | copy-start | bytes 36868
  196.5 61.6 %copy-start.26 = (f32[1,1,3072]{2,1,0:T(1,128)S(1)}, f32[1,1,3072]{2,1,0:T(1,128)}, u32[]{:S(2)}) copy-start(f32[1,1,3072]{2,1,0:T(1,128)} %copy-done.25) | copy-start | bytes 36868
  196.5 61.6 %copy-start.28 = (f32[1,1,3072]{2,1,0:T(1,128)S(1)}, f32[1,1,3072]{2,1,0:T(1,128)}, u32[]{:S(2)}) copy-start(f32[1,1,3072]{2,1,0:T(1,128)} %copy-done.27) | copy-start | bytes 36868
  196.5 61.6 %copy-start.30 = (f32[1,1,3072]{2,1,0:T(1,128)S(1)}, f32[1,1,3072]{2,1,0:T(1,128)}, u32[]{:S(2)}) copy-start(f32[1,1,3072]{2,1,0:T(1,128)} %copy-done.29) | copy-start | bytes 36868
  196.5 61.6 %copy-start.32 = (f32[1,1,3072]{2,1,0:T(1,128)S(1)}, f32[1,1,3072]{2,1,0:T(1,128)}, u32[]{:S(2)}) copy-start(f32[1,1,3072]{2,1,0:T(1,128)} %copy-done.31) | copy-start | bytes 36868
  196.5 61.6 %copy-start.34 = (f32[1,1,3072]{2,1,0:T(1,128)S(1)}, f32[1,1,3072]{2,1,0:T(1,128)}, u32[]{:S(2)}) copy-start(f32[1,1,3072]{2,1,0:T(1,128)} %copy-done.33) | copy-start | bytes 36868
  196.5 61.6 %copy-start.36 = (f32[1,1,3072]{2,1,0:T(1,128)S(1)}, f32[1,1,3072]{2,1,0:T(1,128)}, u32[]{:S(2)}) copy-start(f32[1,1,3072]{2,1,0:T(1,128)} %copy-done.35) | copy-start | bytes 36868
  196.5 61.6 %copy-start.38 = (f32[1,1,3072]{2,1,0:T(1,128)S(1)}, f32[1,1,3072]{2,1,0:T(1,128)}, u32[]{:S(2)}) copy-start(f32[1,1,3072]{2,1,0:T(1,128)} %copy-done.37) | copy-start | bytes 36868
  196.5 61.6 %copy-start.40 = (f32[1,1,3072]{2,1,0:T(1,128)S(1)}, f32[1,1,3072]{2,1,0:T(1,128)}, u32[]{:S(2)}) copy-start(f32[1,1,3072]{2,1,0:T(1,128)} %copy-done.39) | copy-start | bytes 36868
  196.5 61.6 %copy-start.42 = (f32[1,1,3072]{2,1,0:T(1,128)S(1)}, f32[1,1,3072]{2,1,0:T(1,128)}, u32[]{:S(2)}) copy-start(f32[1,1,3072]{2,1,0:T(1,128)} %copy-done.41) | copy-start | bytes 36868
  196.5 61.6 %copy-start.44 = (f32[1,1,3072]{2,1,0:T(1,128)S(1)}, f32[1,1,3072]{2,1,0:T(1,128)}, u32[]{:S(2)}) copy-start(f32[1,1,3072]{2,1,0:T(1,128)} %copy-done.43) | copy-start | bytes 36868
  196.6 61.6 %copy-start.46 = (f32[1,1,3072]{2,1,0:T(1,128)S(1)}, f32[1,1,3072]{2,1,0:T(1,128)}, u32[]{:S(2)}) copy-start(f32[1,1,3072]{2,1,0:T(1,128)} %copy-done.45) | copy-start | bytes 36868
  196.6 61.6 %copy-start.48 = (f32[1,1,3072]{2,1,0:T(1,128)S(1)}, f32[1,1,3072]{2,1,0:T(1,128)}, u32[]{:S(2)}) copy-start(f32[1,1,3072]{2,1,0:T(1,128)} %copy-done.47) | copy-start | bytes 36868
  196.6 61.6 %copy-start.50 = (f32[1,1,3072]{2,1,0:T(1,128)S(1)}, f32[1,1,3072]{2,1,0:T(1,128)}, u32[]{:S(2)}) copy-start(f32[1,1,3072]{2,1,0:T(1,128)} %copy-done.49) | copy-start | bytes 36868
  196.6 61.6 %copy-start.52 = (f32[1,1,3072]{2,1,0:T(1,128)S(1)}, f32[1,1,3072]{2,1,0:T(1,128)}, u32[]{:S(2)}) copy-start(f32[1,1,3072]{2,1,0:T(1,128)} %copy-done.51) | copy-start | bytes 36868
  196.6 61.6 %copy-start.54 = (f32[1,1,3072]{2,1,0:T(1,128)S(1)}, f32[1,1,3072]{2,1,0:T(1,128)}, u32[]{:S(2)}) copy-start(f32[1,1,3072]{2,1,0:T(1,128)} %copy-done.53) | copy-start | bytes 36868
  196.6 61.6 %copy-start.56 = (f32[1,1,3072]{2,1,0:T(1,128)S(1)}, f32[1,1,3072]{2,1,0:T(1,128)}, u32[]{:S(2)}) copy-start(f32[1,1,3072]{2,1,0:T(1,128)} %copy-done.55) | copy-start | bytes 36868
  196.6 61.6 %copy-start.58 = (f32[1,1,3072]{2,1,0:T(1,128)S(1)}, f32[1,1,3072]{2,1,0:T(1,128)}, u32[]{:S(2)}) copy-start(f32[1,1,3072]{2,1,0:T(1,128)} %copy-done.57) | copy-start | bytes 36868
  196.6 61.6 %copy-start.60 = (f32[1,1,3072]{2,1,0:T(1,128)S(1)}, f32[1,1,3072]{2,1,0:T(1,128)}, u32[]{:S(2)}) copy-start(f32[1,1,3072]{2,1,0:T(1,128)} %copy-done.59) | copy-start | bytes 36868
  196.6 61.6 %copy-start.62 = (f32[1,1,3072]{2,1,0:T(1,128)S(1)}, f32[1,1,3072]{2,1,0:T(1,128)}, u32[]{:S(2)}) copy-start(f32[1,1,3072]{2,1,0:T(1,128)} %copy-done.61) | copy-start | bytes 36868
  196.6 61.6 %copy-start.64 = (f32[1,1,3072]{2,1,0:T(1,128)S(1)}, f32[1,1,3072]{2,1,0:T(1,128)}, u32[]{:S(2)}) copy-start(f32[1,1,3072]{2,1,0:T(1,128)} %copy-done.63) | copy-start | bytes 36868
  196.7 61.6 %copy-start.66 = (f32[1,1,3072]{2,1,0:T(1,128)S(1)}, f32[1,1,3072]{2,1,0:T(1,128)}, u32[]{:S(2)}) copy-start(f32[1,1,3072]{2,1,0:T(1,128)} %copy-done.65) | copy-start | bytes 36868
  196.7 61.6 %copy-start.68 = (f32[1,1,3072]{2,1,0:T(1,128)S(1)}, f32[1,1,3072]{2,1,0:T(1,128)}, u32[]{:S(2)}) copy-start(f32[1,1,3072]{2,1,0:T(1,128)} %copy-done.67) | copy-start | bytes 36868
  196.7 61.6 %copy-start.70 = (f32[1,1,3072]{2,1,0:T(1,128)S(1)}, f32[1,1,3072]{2,1,0:T(1,128)}, u32[]{:S(2)}) copy-start(f32[1,1,3072]{2,1,0:T(1,128)} %copy-done.69) | copy-start | bytes 36868
  196.7 61.6 %copy-start.72 = (f32[1,1,3072]{2,1,0:T(1,128)S(1)}, f32[1,1,3072]{2,1,0:T(1,128)}, u32[]{:S(2)}) copy-start(f32[1,1,3072]{2,1,0:T(1,128)} %copy-done.71) | copy-start | bytes 36868
  196.7 61.6 %copy-start.74 = (f32[1,1,3072]{2,1,0:T(1,128)S(1)}, f32[1,1,3072]{2,1,0:T(1,128)}, u32[]{:S(2)}) copy-start(f32[1,1,3072]{2,1,0:T(1,128)} %copy-done.73) | copy-start | bytes 36868
  196.7 61.6 %copy-start.76 = (f32[1,1,3072]{2,1,0:T(1,128)S(1)}, f32[1,1,3072]{2,1,0:T(1,128)}, u32[]{:S(2)}) copy-start(f32[1,1,3072]{2,1,0:T(1,128)} %copy-done.75) | copy-start | bytes 36868
  196.7 61.6 %copy-start.78 = (f32[1,1,3072]{2,1,0:T(1,128)S(1)}, f32[1,1,3072]{2,1,0:T(1,128)}, u32[]{:S(2)}) copy-start(f32[1,1,3072]{2,1,0:T(1,128)} %copy-done.77) | copy-start | bytes 36868
  196.7 61.6 %copy-start.80 = (f32[1,1,3072]{2,1,0:T(1,128)S(1)}, f32[1,1,3072]{2,1,0:T(1,128)}, u32[]{:S(2)}) copy-start(f32[1,1,3072]{2,1,0:T(1,128)} %copy-done.79) | copy-start | bytes 36868
  196.7 61.6 %copy-start.82 = (f32[1,1,3072]{2,1,0:T(1,128)S(1)}, f32[1,1,3072]{2,1,0:T(1,128)}, u32[]{:S(2)}) copy-start(f32[1,1,3072]{2,1,0:T(1,128)} %copy-done.81) | copy-start | bytes 36868
  (33 other events, 271.5 us)
Sparse Core Ops, SparseCore 0:
  29.6 38.5 all-gather.4
  71.1 38.5 all-gather.2
  120.2 65.0 reduce-scatter.1
  198.7 89.1 all-reduce.4
where the time goes:
time: 297 us; the launch traced here: 296 us
  waiting for transfers between devices  154 us (52%)
  blocking collectives  58.5 us (20%)
  matrix products  25 us (8%)
  other arithmetic  17.7 us (6%)
  local copies, waits for them, and re-layouts  15.6 us (5%)
  between operations  15.3 us (5%)
  starting transfers between devices  10.4 us (4%)
    psum x1, blocking collectives, on_device(): lax.psum((gain_part, shift_part, kernel_part, bias_part), 'rows')  58.5 us
    reduce_scatter x1, waiting for transfers between devices, on_device(): lax.psum_scatter(contract(act_grad, up_weight, 1, 1), 'rows', scatter_dim...  53.5 us
    all_gather x1, waiting for transfers between devices, on_device(): normed_all = lax.all_gather(normed, 'rows', axis=0, tiled=True)  37.9 us
    all_gather x1, waiting for transfers between devices, on_device(): cot_all = lax.all_gather(cot_scaled, 'rows', axis=0, tiled=True)  37.2 us
    psum x1, waiting for transfers between devices, on_device(): lax.psum((gain_part, shift_part, kernel_part, bias_part), 'rows')  25.3 us
    dot_general x4, matrix products, contract(): lax.dot_general(left, right, (((left_dim,), (right_dim,)), ((), ())), pre...  20.8 us
    ppermute x2, starting transfers between devices, extended(): lax.ppermute(head, axis, [((i + 1) % count, i) for i in range(count)])  9.49 us
  transfers between devices with their start and end apart: 8, of which 4 were waited for; matrix products, arithmetic and copies ran while one was open for 10% of the time, Pallas kernels for 0%

commit v1 on v0

--- a/solution.py
+++ b/solution.py
@@ -114,7 +114,6 @@
         .astype(jnp.bfloat16)
         .reshape(rows_dev * col_count, channels)
     )
-    cot_all = lax.all_gather(cot_scaled, "rows", axis=0, tiled=True)
     near_rows = extended(features, (("rows", 0),), 3)
     padded = pad_columns(near_rows.astype(jnp.float32) * row_mask)
     conv_out = depthwise(padded, depth_kernel, depth_bias, rows_dev, col_count)
@@ -124,7 +123,13 @@
         .astype(jnp.bfloat16)
         .reshape(rows_dev * col_count, channels)
     )
-    normed_all = lax.all_gather(normed, "rows", axis=0, tiled=True)
+    cot_all, normed_all = jnp.split(
+        jax.lax.all_gather(
+            jnp.concatenate([cot_scaled, normed], axis=1), "rows", axis=0, tiled=True
+        ),
+        [cot_scaled.shape[1]],
+        axis=1,
+    )
     pre_act = jnp.dot(normed_all, up_weight, preferred_element_type=jnp.float32) + up_bias
     hidden = gelu_value(pre_act).astype(jnp.bfloat16)
     down_grad = contract(hidden, cot_all, 0, 0)

time: 297 us -> 260 us (0.88)
  waiting for transfers between devices: 154 us -> 125 us
  local copies, waits for them, and re-layouts: 15.6 us -> 12.2 us
    all_gather x2 -> x1, waiting for transfers between devices: 75.1 us -> 44.2 us  [on_device(): jax.lax.all_gather(jnp.concatenate([cot_scaled, normed], axis=1), 'rows',...]
  transfers between devices with their start and end apart: 8 -> 7, of which waited for: 4 -> 3; matrix products, arithmetic and copies ran while one was open for 10% -> 9% of each run, Pallas kernels for 0% -> 0%
where the time goes in v1:
time: 260 us; the launch traced here: 259 us
  waiting for transfers between devices  125 us (48%)
  blocking collectives  58.5 us (22%)
  matrix products  24 us (9%)
  other arithmetic  15.3 us (6%)
  between operations  14.1 us (5%)
  local copies, waits for them, and re-layouts  12.2 us (5%)
  starting transfers between devices  10.4 us (4%)
    psum x1, blocking collectives, on_device(): lax.psum((gain_part, shift_part, kernel_part, bias_part), 'rows')  58.5 us
    reduce_scatter x1, waiting for transfers between devices, on_device(): lax.psum_scatter(contract(act_grad, up_weight, 1, 1), 'rows', scatter_dim...  53 us
    all_gather x1, waiting for transfers between devices, on_device(): jax.lax.all_gather(jnp.concatenate([cot_scaled, normed], axis=1), 'rows',...  44.2 us
    psum x1, waiting for transfers between devices, on_device(): lax.psum((gain_part, shift_part, kernel_part, bias_part), 'rows')  27.4 us
    dot_general x4, matrix products, contract(): lax.dot_general(left, right, (((left_dim,), (right_dim,)), ((), ())), pre...  19.7 us
    ppermute x2, starting transfers between devices, extended(): lax.ppermute(head, axis, [((i + 1) % count, i) for i in range(count)])  9.49 us
  transfers between devices with their start and end apart: 7, of which 3 were waited for; matrix products, arithmetic and copies ran while one was open for 9% of the time, Pallas kernels for 0%

profile of v1, /device:TPU:0, one launch (start us, length us, event | category | flops | bytes accessed | tf_op | source)
XLA Modules:
  0.0 259.1 jit_solution(12837360268014230585)
XLA Ops:
  7.2 0.0 copy-start.3
  7.2 0.0 copy-start.6
  7.2 0.0 all-gather.2.cloned.1.call-start
  7.2 1.0 fusion.122
  8.3 0.5 collective-permute-start
  8.8 5.1 %collective-permute-start.1 = (bf16[3,4,3072]{2,1,0:T(4,128)(2,1)S(1)}, bf16[3,4,3072]{2,1,0:T(4,128)(2,1)S(1)}, u32[]{:S(2)}, u32[]{:S(2)}) collective-permute-start(bf16[3,4,3072]{2,1,0:T(4,128)(2,1)S(1)} %get-tuple-element.121), channel_id=1, source_target_pairs={{1,0},{2,1},{3,2},{4,3},{5,4},{6,5},{7,6},{8,7},{9,8},{10,9},{11,1... | collective-permute-start | bytes 221192 | tf_op jit(solution)/shard_map/ppermute | solution.py:18
  13.8 1.7 fusion.120
  15.5 2.3 fusion.118
  17.8 2.1 fusion.119
  19.9 0.9 fusion.22
  20.9 0.0 copy-start.5
  20.9 0.0 copy-start.7
  21.0 0.0 collective-permute-done
  21.0 0.0 collective-permute-done.1
  21.0 0.0 copy-done.3
  21.0 0.2 convert_multiply_fusion.1
  21.2 0.0 copy-done.6
  21.2 0.0 copy-start.8
  21.2 4.4 %fusion.117 = (f32[4,4]{1,0:T(4,128)S(1)}, f32[4,4,3072]{2,1,0:T(4,128)S(1)}) fusion(f32[3072]{0:T(1024)S(1)} %copy-done.6, f32[3072]{0:T(1024)S(1)} %bitcast.137, f32[3072]{0:T(1024)S(1)} %bitcast.139, f32[3072]{0:T(1024)S(1)} %bitcast.143, f32[10,4,3072]{2,1,0:T(4,128)S(1)} %convert_multiply_fusion.1, f32[3072]{0:T(1024)S(1)} %bitcast.145, ...), kind=kLoop, calls=%fused_computation.287 | loop fusion | flops 4866032 | bytes 2678848 | tf_op jit(solution)/shard_map/reduce_sum | solution.py:72
  25.6 0.2 multiply_reduce_fusion.52
  25.8 0.0 copy-done.5
  25.9 0.1 add_convert_fusion
  26.0 0.7 pad_maximum_fusion
  26.7 0.0 all-gather.2.cloned.1.call-update
  26.7 0.0 reduce-scatter.2.cloned.1.call-start
  26.8 44.2 %all-gather.2.cloned.1.call-done = bf16[256,6144]{1,0:T(8,128)(2,1)} async-done(((bf16[16,6144]{1,0:T(8,128)(2,1)}), bf16[256,6144]{1,0:T(8,128)(2,1)}) %all-gather.2.cloned.1.call-update) | async-done | bytes 3145744 | tf_op jit(solution)/shard_map/all_gather | solution.py:127
  71.0 0.0 copy-done.8
  71.0 4.3 %fusion.11 = f32[256,768]{1,0:T(8,128)S(1)} fusion(bf16[3072,768]{1,0:T(8,128)(2,1)} %param.16, bf16[256,6144]{1,0:T(8,128)(2,1)} %all-gather.2.cloned.1.call-done, f32[768]{0:T(1024)S(1)} %copy-done.8), kind=kOutput, calls=%fused_computation.93 | convolution fusion | flops 1208156160 | bytes 7080960 | tf_op jit(solution)/shard_map/dot_general | solution.py:133
  75.4 0.0 slice-start.1
  75.4 4.6 %convert_reduce_fusion = (f32[768]{0:T(1024)}, bf16[256,768]{1,0:T(8,128)(2,1)S(1)}) fusion(f32[256,768]{1,0:T(8,128)S(1)} %fusion.11, bf16[768,3072]{1,0:T(8,128)(2,1)} %param.18, bf16[256,6144]{1,0:T(8,128)(2,1)S(1)} %copy-done), kind=kOutput, calls=%fused_computation.101 | convolution fusion | flops 1210318080 | bytes 7474176 | tf_op jit(solution)/shard_map/dot_general | solution.py:35
  80.0 3.2 %fusion.123 = f32[256,3072]{1,0:T(8,128)} fusion(bf16[256,768]{1,0:T(8,128)(2,1)S(1)} %get-tuple-element.123, bf16[3072,768]{1,0:T(8,128)(2,1)S(1)} %bitcast.118), kind=kOutput, calls=%fused_computation.293 | convolution fusion | flops 1207959552 | bytes 8257536 | tf_op jit(solution)/shard_map/dot_general | solution.py:35
  83.1 0.0 reduce-scatter.2.cloned.1.call-update
  83.1 0.2 all-reduce.5.cloned.1.call-start
  83.4 6.7 %fusion = f32[3072,768]{1,0:T(8,128)} fusion(bf16[256,768]{1,0:T(8,128)(2,1)S(1)} %get-tuple-element.123, bf16[256,6144]{1,0:T(8,128)(2,1)} %all-gather.2.cloned.1.call-done), kind=kOutput, calls=%fused_computation.84 | convolution fusion | flops 1207959552 | bytes 11403264 | tf_op jit(solution)/shard_map/dot_general | solution.py:35
  90.1 0.0 copy-done.1
  90.1 5.2 %fusion.4 = f32[768,3072]{1,0:T(8,128)} fusion(bf16[256,6144]{1,0:T(8,128)(2,1)S(1)} %copy-done.1, f32[256,768]{1,0:T(8,128)S(1)} %fusion.11), kind=kOutput, calls=%fused_computation.88 | convolution fusion | flops 1208942592 | bytes 11796480 | tf_op jit(solution)/shard_map/dot_general | solution.py:35
  95.3 53.0 %reduce-scatter.2.cloned.1.call-done = f32[16,3072]{1,0:T(8,128)} async-done(((f32[256,3072]{1,0:T(8,128)}), f32[16,3072]{1,0:T(8,128)}) %reduce-scatter.2.cloned.1.call-update) | async-done | bytes 196624 | tf_op jit(solution)/shard_map/reduce_scatter | solution.py:140
  148.3 1.1 fusion.116
  149.4 0.1 div.44
  149.5 1.0 reshape.91
  150.5 0.3 multiply_reduce_fusion
  150.7 1.5 multiply_reduce_fusion.1
  152.2 1.0 multiply_reduce_fusion.37
  153.3 1.3 multiply_reduce_fusion.19
  154.7 0.1 collective-permute-start.2
  154.7 4.4 %collective-permute-start.3 = (bf16[3,4,3072]{2,1,0:T(4,128)(2,1)S(1)}, bf16[3,4,3072]{2,1,0:T(4,128)(2,1)S(1)}, u32[]{:S(2)}, u32[]{:S(2)}) collective-permute-start(bf16[3,4,3072]{2,1,0:T(4,128)(2,1)S(1)} %get-tuple-element.119), channel_id=1, source_target_pairs={{1,0},{2,1},{3,2},{4,3},{5,4},{6,5},{7,6},{8,7},{9,8},{10,9},{11,1... | collective-permute-start | bytes 221192 | tf_op jit(solution)/shard_map/ppermute | solution.py:18
  159.2 0.1 stack.199
  159.3 0.0 copy-start.4
  159.3 0.1 stack.208
  159.5 0.1 stack.217
  159.6 0.1 stack.226
  159.8 0.1 stack.235
  160.0 0.1 stack.244
  160.1 0.1 stack.253
  160.3 0.0 copy-start.2
  160.3 0.8 copy-done.2
  161.1 0.0 all-reduce.5.cloned.1.call-update
  161.2 58.5 %all-reduce.2 = (f32[3072]{0:T(1024)}, f32[3072]{0:T(1024)}, f32[3072]{0:T(1024)}) all-reduce(f32[3072]{0:T(1024)S(1)} %get-tuple-element.61, f32[3072]{0:T(1024)S(1)} %get-tuple-element.57, f32[3072]{0:T(1024)S(1)} %get-tuple-element.59), channel_id=1, replica_groups=mesh['groups'=2,'rows'=16] {'rows'}, use_global_device_ids=true, to_apply=%region_57.58 | all-reduce | flops 9216 | bytes 73728 | tf_op jit(solution)/shard_map/psum | solution.py:164
  219.7 0.0 collective-permute-done.2
  219.7 0.0 collective-permute-done.3
  219.7 0.2 convert_multiply_fusion
  219.9 3.3 %fusion.23 = bf16[4,4,3072]{2,1,0:T(4,128)(2,1)} fusion(bf16[4,4,3072]{2,1,0:T(4,128)(2,1)S(1)} %copy-done.4, f32[10,4,3072]{2,1,0:T(4,128)S(1)} %convert_multiply_fusion, f32[3072]{0:T(1024)S(1)} %bitcast.138, f32[3072]{0:T(1024)S(1)} %bitcast.140, f32[3072]{0:T(1024)S(1)} %bitcast.144, f32[3072]{0:T(1024)S(1)} %bitcast.146, f32[3072]{0:T(1024)S(1)} %bitcast.148, ...), kind=kLoop, calls=%fused_computation.109 | loop fusion | flops 4915200 | bytes 2666496 | tf_op jit(solution)/shard_map/convert_element_type | solution.py:163
  223.2 27.4 %all-reduce.5.cloned.1.call-done = f32[7,7,3072]{2,1,0:T(8,128)} async-done(((f32[7,7,3072]{2,1,0:T(8,128)}), f32[7,7,3072]{2,1,0:T(8,128)}) %all-reduce.5.cloned.1.call-update) | async-done | bytes 602128 | tf_op jit(solution)/shard_map/psum | solution.py:164
  250.6 2.0 copy.25
  (24 shorter events, 0.2 us)
Async XLA Ops:
  7.2 13.8 %copy-start.3 = (bf16[4,4,3072]{2,1,0:T(4,128)(2,1)S(1)}, bf16[4,4,3072]{2,1,0:T(4,128)(2,1)}, u32[]{:S(2)}) copy-start(bf16[4,4,3072]{2,1,0:T(4,128)(2,1)} %param.10) | copy-start | bytes 294916
  7.2 14.0 %copy-start.6 = (f32[3072]{0:T(1024)S(1)}, f32[3072]{0:T(1024)}, u32[]{:S(2)}) copy-start(f32[3072]{0:T(1024)} %param.13) | copy-start | bytes 36868
  7.2 63.8 %all-gather.2.cloned.1.call-start = ((), (), s32[]{:S(2)}) async-start(), calls=%async_computation.1 | async-start | bytes 3342336 | tf_op jit(solution)/shard_map/all_gather | solution.py:127
  8.3 12.7 %collective-permute-start = (bf16[3,4,3072]{2,1,0:T(4,128)(2,1)S(1)}, bf16[3,4,3072]{2,1,0:T(4,128)(2,1)S(1)}, u32[]{:S(2)}, u32[]{:S(2)}) collective-permute-start(bf16[3,4,3072]{2,1,0:T(4,128)(2,1)S(1)} %get-tuple-element.120), channel_id=1, source_target_pairs={{0,1},{1,2},{2,3},{3,4},{4,5},{5,6},{6,7},{7,8},{8,9},{9,10},{10,1... | collective-permute-start | bytes 221192 | tf_op jit(solution)/shard_map/ppermute | solution.py:16
  8.8 12.2 %collective-permute-start.1 = (bf16[3,4,3072]{2,1,0:T(4,128)(2,1)S(1)}, bf16[3,4,3072]{2,1,0:T(4,128)(2,1)S(1)}, u32[]{:S(2)}, u32[]{:S(2)}) collective-permute-start(bf16[3,4,3072]{2,1,0:T(4,128)(2,1)S(1)} %get-tuple-element.121), channel_id=1, source_target_pairs={{1,0},{2,1},{3,2},{4,3},{5,4},{6,5},{7,6},{8,7},{9,8},{10,9},{11,1... | collective-permute-start | bytes 221192 | tf_op jit(solution)/shard_map/ppermute | solution.py:18
  20.9 5.0 %copy-start.5 = (f32[3072]{0:T(1024)S(1)}, f32[3072]{0:T(1024)}, u32[]{:S(2)}) copy-start(f32[3072]{0:T(1024)} %param.14) | copy-start | bytes 36868
  20.9 4.9 %copy-start.7 = (f32[3072]{0:T(1024)S(1)}, f32[3072]{0:T(1024)}, u32[]{:S(2)}) copy-start(f32[3072]{0:T(1024)} %param.15) | copy-start | bytes 36868
  21.2 49.8 %copy-start.8 = (f32[768]{0:T(1024)S(1)}, f32[768]{0:T(1024)}, u32[]{:S(2)}) copy-start(f32[768]{0:T(1024)} %param.17) | copy-start | bytes 9220
  26.7 121.6 %reduce-scatter.2.cloned.1.call-start = ((), (), s32[]{:S(2)}) async-start(), calls=%async_computation.2 | async-start | bytes 3342336 | tf_op jit(solution)/shard_map/reduce_scatter | solution.py:140
  71.0 4.3 %copy-start = (bf16[256,6144]{1,0:T(8,128)(2,1)S(1)}, bf16[256,6144]{1,0:T(8,128)(2,1)}, u32[]{:S(2)}) copy-start(bf16[256,6144]{1,0:T(8,128)(2,1)} %all-gather.2.cloned.1.call-done) | copy-start | bytes 9437188
  71.0 8.9 %slice-start = ((s8[4718592]{0:T(1024)(128)(4,1)}), s8[4194304]{0:T(1024)(128)(4,1)S(1)}, s32[]{:S(2)}) async-start(s8[4718592]{0:T(1024)(128)(4,1)} %bitcast.117), calls=%async_computation.4 | async-start | bytes 8388608
  75.4 4.6 %slice-start.1 = ((s8[4718592]{0:T(1024)(128)(4,1)}), s8[524288]{0:T(1024)(128)(4,1)S(1)}, s32[]{:S(2)}) async-start(s8[4718592]{0:T(1024)(128)(4,1)} %bitcast.117), calls=%async_computation.5 | async-start | bytes 1048576
  83.1 167.5 %all-reduce.5.cloned.1.call-start = ((), (), s32[]{:S(2)}) async-start(), calls=%async_computation.3 | async-start | bytes 1376256 | tf_op jit(solution)/shard_map/psum | solution.py:164
  83.4 6.8 %copy-start.1 = (bf16[256,6144]{1,0:T(8,128)(2,1)S(1)}, bf16[256,6144]{1,0:T(8,128)(2,1)}, u32[]{:S(2)}) copy-start(bf16[256,6144]{1,0:T(8,128)(2,1)} %all-gather.2.cloned.1.call-done) | copy-start | bytes 9437188
  154.7 65.0 %collective-permute-start.2 = (bf16[3,4,3072]{2,1,0:T(4,128)(2,1)S(1)}, bf16[3,4,3072]{2,1,0:T(4,128)(2,1)S(1)}, u32[]{:S(2)}, u32[]{:S(2)}) collective-permute-start(bf16[3,4,3072]{2,1,0:T(4,128)(2,1)S(1)} %get-tuple-element.118), channel_id=1, source_target_pairs={{0,1},{1,2},{2,3},{3,4},{4,5},{5,6},{6,7},{7,8},{8,9},{9,10},{10,1... | collective-permute-start | bytes 221192 | tf_op jit(solution)/shard_map/ppermute | solution.py:16
  154.7 64.9 %collective-permute-start.3 = (bf16[3,4,3072]{2,1,0:T(4,128)(2,1)S(1)}, bf16[3,4,3072]{2,1,0:T(4,128)(2,1)S(1)}, u32[]{:S(2)}, u32[]{:S(2)}) collective-permute-start(bf16[3,4,3072]{2,1,0:T(4,128)(2,1)S(1)} %get-tuple-element.119), channel_id=1, source_target_pairs={{1,0},{2,1},{3,2},{4,3},{5,4},{6,5},{7,6},{8,7},{9,8},{10,9},{11,1... | collective-permute-start | bytes 221192 | tf_op jit(solution)/shard_map/ppermute | solution.py:18
  159.3 60.6 %copy-start.4 = (bf16[4,4,3072]{2,1,0:T(4,128)(2,1)S(1)}, bf16[4,4,3072]{2,1,0:T(4,128)(2,1)}, u32[]{:S(2)}) copy-start(bf16[4,4,3072]{2,1,0:T(4,128)(2,1)} %param.11) | copy-start | bytes 294916
  160.3 0.8 copy-start.2
Sparse Core Ops, SparseCore 0:
  26.9 44.1 all-gather.1
  83.3 65.0 reduce-scatter.1
  161.3 89.2 all-reduce.4
